TPU v7x, 32 devices: a whole 2x2x4 slice. The times are simulated.
32 devices in a mesh: dp: 4 (over y, x), seq: 8 (over z, core).
Axes of the slice: x: 2, y: 2, z: 4, core: 2. Of those that a mesh axis runs over, the one named last changes fastest.
Arguments:
- q_arrive: bfloat16 [4, 1024, 2048], P('dp', 'seq'), may hold values from -6 to 6
- k_arrive: bfloat16 [4, 1024, 2048], P('dp', 'seq'), may hold values from -6 to 6
- v_arrive: bfloat16 [4, 1024, 2048], P('dp', 'seq'), may hold values from -6 to 6
- source_rank: int32 [4, 256], P(None, 'seq'), may hold values from 0 to 3, as said below
- first_length: int32 [4], replicated, may hold values from 1 to 1023
- filter_taps: bfloat16 [1024, 2048], P('seq'), may hold values from -2 to 2
Outputs:
- operator_out: bfloat16 [4, 1024, 2048], P('dp', 'seq')
Inputs may be any that keep to these rules, and one draw needn't show every extreme that they name: For each block position b, source_rank[:, b] is a permutation of the 4 data indices. Of the 32 blocks of one device along seq, at most 16 of one pack come from one source index, and some pair reaches 16.
All inputs are finite; a program needn't handle non-finite values.
Results may differ from a plain program's by a relative error of at most 0.005.
Values may be sent and summed in bfloat16 or wider, within the bound.
A program may use at most 64 MiB of HBM per device.

v0:
```python
import math

import jax
import jax.numpy as jnp
from jax import lax
from jax.sharding import PartitionSpec as P


def angles(first_ids, second_ids, period):
    return (
        2.0
        * math.pi
        / period
        * (first_ids[:, None] * second_ids[None, :] % period).astype(jnp.float32)
    )


def apply_table(matrix, values):
    return jnp.einsum("ab,brx->arx", matrix, values, precision=lax.Precision.HIGH)


def along_middle(matrix, values):
    return jnp.einsum("km,jmx->jkx", matrix, values, precision=lax.Precision.HIGHEST)


def complex_apply(helper, matrix_real, matrix_imag, real_part, imag_part):
    out_real = helper(matrix_real, real_part) - helper(matrix_imag, imag_part)
    out_imag = helper(matrix_imag, real_part) + helper(matrix_real, imag_part)
    return (out_real, out_imag)


def body(q_arrive, k_arrive, v_arrive, source_rank, first_length, filter_taps):
    groups = lax.axis_size("dp")
    shards = lax.axis_size("seq")
    group_index = lax.axis_index("dp")
    shard_index = lax.axis_index("seq")
    tokens_here = q_arrive.shape[1]
    channels = q_arrive.shape[2]
    blocks_here = source_rank.shape[1]
    block_len = tokens_here // blocks_here
    capacity = max(2, 2 * blocks_here // groups)
    slot_ids = jnp.arange(capacity, dtype=jnp.int32)
    outgoing_mask = (source_rank == group_index).astype(jnp.int32)
    send_slot = jnp.cumsum(outgoing_mask, axis=1) - outgoing_mask
    send_pick = (outgoing_mask[:, None, :] == 1) & (
        send_slot[:, None, :] == slot_ids[None, :, None]
    )
    send_pick = send_pick.astype(jnp.bfloat16).reshape(groups * capacity, blocks_here)
    own_source = lax.dynamic_slice_in_dim(source_rank, group_index, 1, 0)[0]
    block_ids = jnp.arange(blocks_here, dtype=jnp.int32)
    earlier_same = (own_source[:, None] == own_source[None, :]) & (
        block_ids[None, :] < block_ids[:, None]
    )
    receive_slot = jnp.sum(earlier_same.astype(jnp.int32), axis=1)
    group_ids = jnp.arange(groups, dtype=jnp.int32)
    receive_pick = (own_source[:, None, None] == group_ids[None, :, None]) & (
        receive_slot[:, None, None] == slot_ids[None, None, :]
    )
    receive_pick = receive_pick.astype(jnp.bfloat16).reshape(blocks_here, groups * capacity)
    queries_in = q_arrive[0]
    payload = jnp.concatenate([queries_in, k_arrive[0], v_arrive[0]], axis=1)
    row_width = payload.shape[1]
    outgoing = jnp.dot(
        send_pick,
        payload.reshape(blocks_here, block_len * row_width),
        preferred_element_type=jnp.float32,
    )
    outgoing = outgoing.astype(jnp.bfloat16).reshape(groups, capacity * block_len, row_width)
    arrived = lax.all_to_all(outgoing, "dp", split_axis=0, concat_axis=0, tiled=True)
    packed = jnp.dot(
        receive_pick,
        arrived.reshape(groups * capacity, block_len * row_width),
        preferred_element_type=jnp.float32,
    )
    packed = packed.astype(jnp.bfloat16).reshape(tokens_here, row_width)
    queries = packed[:, :channels]
    product = (
        packed[:, channels : 2 * channels].astype(jnp.float32)
        * packed[:, 2 * channels :].astype(jnp.float32)
    ).astype(jnp.bfloat16)
    boundary = lax.dynamic_slice_in_dim(first_length, group_index, 1, 0)[0]
    positions = shard_index * tokens_here + jnp.arange(tokens_here, dtype=jnp.int32)
    second_part = jnp.where((positions >= boundary)[:, None], product, jnp.zeros_like(product))
    filter_width = filter_taps.shape[1]
    block_rows = tokens_here // shards
    signal = jnp.concatenate([product, second_part], axis=1).reshape(
        shards, block_rows, 2 * channels
    )
    signal_cols, filter_cols = (
        lax.all_to_all(signal, "seq", split_axis=0, concat_axis=0, tiled=True),
        lax.all_to_all(
            filter_taps.reshape(shards, block_rows, filter_width),
            "seq",
            split_axis=0,
            concat_axis=0,
            tiled=True,
        ),
    )
    freq_count = 2 * shards
    length = freq_count * tokens_here
    freq_ids = jnp.arange(freq_count, dtype=jnp.int32)
    piece_ids = jnp.arange(shards, dtype=jnp.int32)
    outer_angle = angles(freq_ids, piece_ids, freq_count)
    outer_real = jnp.cos(outer_angle)
    outer_imag = -jnp.sin(outer_angle)
    local_ids = shard_index * block_rows + jnp.arange(block_rows, dtype=jnp.int32)
    twiddle = angles(freq_ids, local_ids, length)
    twiddle_real = jnp.cos(twiddle)[:, :, None]
    twiddle_imag = -jnp.sin(twiddle)[:, :, None]
    data_real = signal_cols[:, :, :channels].astype(jnp.float32)
    data_imag = signal_cols[:, :, channels:].astype(jnp.float32)
    section_real, section_imag = complex_apply(
        apply_table, outer_real, outer_imag, data_real, data_imag
    )
    signal_real = section_real * twiddle_real - section_imag * twiddle_imag
    signal_imag = section_real * twiddle_imag + section_imag * twiddle_real
    filter_values = filter_cols.astype(jnp.float32)
    filter_section_real = apply_table(outer_real, filter_values)
    filter_section_imag = apply_table(outer_imag, filter_values)
    filter_real = filter_section_real * twiddle_real - filter_section_imag * twiddle_imag
    filter_imag = filter_section_real * twiddle_imag + filter_section_imag * twiddle_real
    signal_freq, filter_freq = (
        lax.all_to_all(
            jnp.concatenate([signal_real, signal_imag], axis=2),
            "seq",
            split_axis=0,
            concat_axis=1,
            tiled=True,
        ),
        lax.all_to_all(
            jnp.concatenate([filter_real, filter_imag], axis=2),
            "seq",
            split_axis=0,
            concat_axis=1,
            tiled=True,
        ),
    )
    token_ids = jnp.arange(tokens_here, dtype=jnp.int32)
    inner_angle = angles(token_ids, token_ids, tokens_here)
    inner_real = jnp.cos(inner_angle)
    inner_imag = -jnp.sin(inner_angle)
    spectrum_real, spectrum_imag = complex_apply(
        along_middle,
        inner_real,
        inner_imag,
        signal_freq[:, :, :channels],
        signal_freq[:, :, channels:],
    )
    response_real, response_imag = complex_apply(
        along_middle,
        inner_real,
        inner_imag,
        filter_freq[:, :, :filter_width],
        filter_freq[:, :, filter_width:],
    )
    joint_real = spectrum_real * response_real - spectrum_imag * response_imag
    joint_imag = spectrum_real * response_imag + spectrum_imag * response_real
    back_real, back_imag = complex_apply(
        along_middle, inner_real, -inner_imag, joint_real, joint_imag
    )
    returned = lax.all_to_all(
        jnp.concatenate([back_real, back_imag], axis=2),
        "seq",
        split_axis=1,
        concat_axis=0,
        tiled=True,
    )
    returned_real = returned[:, :, :channels]
    returned_imag = returned[:, :, channels:]
    untwist_real = returned_real * twiddle_real + returned_imag * twiddle_imag
    untwist_imag = returned_imag * twiddle_real - returned_real * twiddle_imag
    final_angle = angles(piece_ids, freq_ids, freq_count)
    final_real = jnp.cos(final_angle) / length
    final_imag = jnp.sin(final_angle) / length
    conv_real, conv_imag = complex_apply(
        apply_table, final_real, final_imag, untwist_real, untwist_imag
    )
    pack_positions = piece_ids[:, None] * tokens_here + local_ids[None, :]
    response = jnp.where((pack_positions >= boundary)[:, :, None], conv_imag, conv_real)
    arranged = lax.all_to_all(response, "seq", split_axis=0, concat_axis=1, tiled=True)
    result = (queries.astype(jnp.float32) * arranged[0]).astype(jnp.bfloat16)
    return result.reshape(1, tokens_here, channels)


def solution(mesh):
    return jax.shard_map(
        body,
        mesh=mesh,
        in_specs=(
            P("dp", "seq", None),
            P("dp", "seq", None),
            P("dp", "seq", None),
            P(None, "seq"),
            P(),
            P("seq", None),
        ),
        out_specs=P("dp", "seq", None),
        check_vma=False,
    )
```

profile of v0, /device:TPU:1, one launch (start us, length us, event | category | flops | bytes accessed | tf_op | source)
XLA Modules:
  0.0 510.1 jit_solution(7814701173654378851)
XLA Ops:
  0.9 1.5 pad_maximum_fusion.3
  2.4 2.2 reshape.223
  4.6 2.4 convolution_convert_fusion
  6.9 3.7 reshape.224
  10.6 4.4 all-to-all-start
  17.1 33.4 %all-to-all-done = bf16[4,64,6144]{2,1,0:T(8,128)(2,1)S(1)} async-done(((bf16[4,64,6144]{2,1,0:T(8,128)(2,1)}), bf16[4,64,6144]{2,1,0:T(8,128)(2,1)S(1)}, u32[]{:S(2)}, u32[]{:S(2)}) %all-to-all-start) | async-done | bytes 3145760 | tf_op jit(solution)/shard_map/all_to_all | solution.py:69
  50.6 6.6 %all-to-all-start.3 = ((bf16[8,16,2048]{2,1,0:T(8,128)(2,1)}), bf16[8,16,2048]{2,1,0:T(8,128)(2,1)}, u32[]{:S(2)}, u32[]{:S(2)}) async-start(bf16[8,16,2048]{2,1,0:T(8,128)(2,1)} %bitcast.111), calls=%async_computation.3 | async-start | bytes 1048576 | tf_op jit(solution)/shard_map/all_to_all | solution.py:91
  57.2 3.7 reshape.225
  60.8 2.5 convolution_convert_fusion.1
  63.3 1.3 reshape.226
  64.8 1.3 pad_maximum_fusion.4
  66.1 5.6 %all-to-all-done.3 = bf16[8,16,2048]{2,1,0:T(8,128)(2,1)} async-done(((bf16[8,16,2048]{2,1,0:T(8,128)(2,1)}), bf16[8,16,2048]{2,1,0:T(8,128)(2,1)}, u32[]{:S(2)}, u32[]{:S(2)}) %all-to-all-start.3) | async-done | bytes 524320 | tf_op jit(solution)/shard_map/all_to_all | solution.py:91
  71.8 4.8 all-to-all-start.1
  76.7 1.9 fusion.30
  78.6 23.7 %all-to-all-done.1 = bf16[8,16,4096]{2,1,0:T(8,128)(2,1)S(1)} async-done(((bf16[8,16,4096]{2,1,0:T(8,128)(2,1)}), bf16[8,16,4096]{2,1,0:T(8,128)(2,1)S(1)}, u32[]{:S(2)}, u32[]{:S(2)}) %all-to-all-start.1) | async-done | bytes 1048608 | tf_op jit(solution)/shard_map/all_to_all | solution.py:90
  105.9 4.8 multiply_subtract_fusion.2
  111.1 4.4 copy.59
  115.5 5.4 %all-to-all-start.4 = ((f32[16,16,4096]{2,1,0:T(8,128)}), f32[16,16,4096]{2,1,0:T(8,128)}, u32[]{:S(2)}, u32[]{:S(2)}) async-start(f32[16,16,4096]{2,1,0:T(8,128)} %copy.59), calls=%async_computation.4 | async-start | bytes 8388608 | tf_op jit(solution)/shard_map/all_to_all | solution.py:130
  121.0 1.9 pad_maximum_fusion
  122.9 4.4 copy.53
  127.3 86.9 %all-to-all-done.4 = f32[16,16,4096]{2,1,0:T(8,128)} async-done(((f32[16,16,4096]{2,1,0:T(8,128)}), f32[16,16,4096]{2,1,0:T(8,128)}, u32[]{:S(2)}, u32[]{:S(2)}) %all-to-all-start.4) | async-done | bytes 4194336 | tf_op jit(solution)/shard_map/all_to_all | solution.py:130
  214.2 5.5 %all-to-all-start.2 = ((f32[16,16,4096]{2,1,0:T(8,128)}), f32[16,16,4096]{2,1,0:T(8,128)}, u32[]{:S(2)}, u32[]{:S(2)}) async-start(f32[16,16,4096]{2,1,0:T(8,128)} %copy.53), calls=%async_computation.2 | async-start | bytes 8388608 | tf_op jit(solution)/shard_map/all_to_all | solution.py:123
  219.7 2.5 copy.60
  222.2 4.9 fusion.11
  227.1 3.5 fusion.13
  230.7 82.2 %all-to-all-done.2 = f32[16,16,4096]{2,1,0:T(8,128)} async-done(((f32[16,16,4096]{2,1,0:T(8,128)}), f32[16,16,4096]{2,1,0:T(8,128)}, u32[]{:S(2)}, u32[]{:S(2)}) %all-to-all-start.2) | async-done | bytes 4194336 | tf_op jit(solution)/shard_map/all_to_all | solution.py:123
  312.8 2.5 copy.54
  315.3 3.6 fusion.17
  318.9 3.8 fusion.19
  322.7 3.7 convolution_subtract_fusion.1
  326.3 3.7 convolution_add_fusion.1
  330.0 4.0 convolution_subtract_fusion.2
  334.1 3.7 multiply_add_fusion.1
  337.8 2.1 fusion.5
  339.9 2.1 fusion.7
  342.1 2.2 fusion.1
  344.3 2.1 fusion
  346.4 2.3 pad_maximum_fusion.2
  348.6 7.3 %copy.63 = f32[2,128,4096]{2,0,1:T(2,128)} copy(f32[2,128,4096]{1,2,0:T(8,128)} %pad_maximum_fusion.2) | data formatting | bytes 8388608 | tf_op jit(solution)/shard_map/concatenate | solution.py:162
  355.9 5.3 %all-to-all-start.5 = ((f32[2,128,4096]{2,0,1:T(2,128)}), f32[2,128,4096]{2,0,1:T(2,128)}, u32[]{:S(2)}, u32[]{:S(2)}) async-start(f32[2,128,4096]{2,0,1:T(2,128)} %copy.63), calls=%async_computation.5 | async-start | bytes 8388608 | tf_op jit(solution)/shard_map/all_to_all | solution.py:161
  361.9 92.5 %all-to-all-done.5 = f32[2,128,4096]{2,0,1:T(2,128)} async-done(((f32[2,128,4096]{2,0,1:T(2,128)}), f32[2,128,4096]{2,0,1:T(2,128)}, u32[]{:S(2)}, u32[]{:S(2)}) %all-to-all-start.5) | async-done | bytes 4194336 | tf_op jit(solution)/shard_map/all_to_all | solution.py:161
  454.5 4.6 copy.64
  459.1 5.2 %copy.65 = f32[8,2,16,4096]{3,1,0,2:T(2,128)} copy(f32[8,2,16,4096]{3,2,0,1:T(8,128)S(1)} %bitcast.109) | data formatting | bytes 8388608 | tf_op jit(solution)/shard_map/all_to_all | solution.py:161
  464.3 6.1 %all_to_all.69 = f32[16,16,4096]{2,0,1:T(8,128)} reshape(f32[8,2,16,4096]{3,1,0,2:T(2,128)} %copy.65) | data formatting | bytes 8388608 | tf_op jit(solution)/shard_map/all_to_all | solution.py:161
  470.4 3.2 fusion.32
  473.6 3.1 fusion.33
  479.1 28.8 %all_to_all.78 = f32[8,16,2048]{2,1,0:T(8,128)S(1)} all-to-all(f32[8,16,2048]{2,1,0:T(8,128)S(1)} %copy.66), channel_id=1, replica_groups=mesh['dp'=4,'seq'=8] {'seq'}, dimensions={0} | all-to-all | bytes 2097152 | tf_op jit(solution)/shard_map/all_to_all | solution.py:180
  507.9 2.0 fusion.21
  (39 shorter events, 10.4 us)
Async XLA Ops:
  10.6 4.4 copy-start.6
  10.6 40.0 %all-to-all-start = ((bf16[4,64,6144]{2,1,0:T(8,128)(2,1)}), bf16[4,64,6144]{2,1,0:T(8,128)(2,1)S(1)}, u32[]{:S(2)}, u32[]{:S(2)}) async-start(bf16[4,64,6144]{2,1,0:T(8,128)(2,1)} %reshape.224), calls=%async_computation | async-start | bytes 6291456 | tf_op jit(solution)/shard_map/all_to_all | solution.py:69
  50.6 21.2 %all-to-all-start.3 = ((bf16[8,16,2048]{2,1,0:T(8,128)(2,1)}), bf16[8,16,2048]{2,1,0:T(8,128)(2,1)}, u32[]{:S(2)}, u32[]{:S(2)}) async-start(bf16[8,16,2048]{2,1,0:T(8,128)(2,1)} %bitcast.111), calls=%async_computation.3 | async-start | bytes 1048576 | tf_op jit(solution)/shard_map/all_to_all | solution.py:91
  64.6 1.5 copy-start.5
  71.8 30.5 %all-to-all-start.1 = ((bf16[8,16,4096]{2,1,0:T(8,128)(2,1)}), bf16[8,16,4096]{2,1,0:T(8,128)(2,1)S(1)}, u32[]{:S(2)}, u32[]{:S(2)}) async-start(bf16[8,16,4096]{2,1,0:T(8,128)(2,1)} %bitcast.110), calls=%async_computation.1 | async-start | bytes 2097152 | tf_op jit(solution)/shard_map/all_to_all | solution.py:90
  115.5 5.4 %copy-start.4 = (f32[16,16,2048]{2,0,1:T(8,128)S(1)}, f32[16,16,2048]{2,0,1:T(8,128)}, u32[]{:S(2)}) copy-start(f32[16,16,2048]{2,0,1:T(8,128)} %get-tuple-element.17) | copy-start | bytes 6291460
  115.5 98.7 %all-to-all-start.4 = ((f32[16,16,4096]{2,1,0:T(8,128)}), f32[16,16,4096]{2,1,0:T(8,128)}, u32[]{:S(2)}, u32[]{:S(2)}) async-start(f32[16,16,4096]{2,1,0:T(8,128)} %copy.59), calls=%async_computation.4 | async-start | bytes 8388608 | tf_op jit(solution)/shard_map/all_to_all | solution.py:130
  214.2 98.6 %all-to-all-start.2 = ((f32[16,16,4096]{2,1,0:T(8,128)}), f32[16,16,4096]{2,1,0:T(8,128)}, u32[]{:S(2)}, u32[]{:S(2)}) async-start(f32[16,16,4096]{2,1,0:T(8,128)} %copy.53), calls=%async_computation.2 | async-start | bytes 8388608 | tf_op jit(solution)/shard_map/all_to_all | solution.py:123
  222.2 4.9 copy-start
  315.3 7.4 %copy-start.3 = (f32[2,2048,128]{2,1,0:T(8,128)S(1)}, f32[2,2048,128]{2,1,0:T(8,128)}, u32[]{:S(2)}) copy-start(f32[2,2048,128]{2,1,0:T(8,128)} %fusion.11) | copy-start | bytes 6291460
  318.9 3.8 copy-start.1
  355.9 98.6 %all-to-all-start.5 = ((f32[2,128,4096]{2,0,1:T(2,128)}), f32[2,128,4096]{2,0,1:T(2,128)}, u32[]{:S(2)}, u32[]{:S(2)}) async-start(f32[2,128,4096]{2,0,1:T(2,128)} %copy.63), calls=%async_computation.5 | async-start | bytes 8388608 | tf_op jit(solution)/shard_map/all_to_all | solution.py:161
  470.4 6.3 %copy-start.2 = (f32[16,16,4096]{2,0,1:T(8,128)S(1)}, f32[16,16,4096]{2,0,1:T(8,128)}, u32[]{:S(2)}) copy-start(f32[16,16,4096]{2,0,1:T(8,128)} %all_to_all.69) | copy-start | bytes 12582916
where the time goes:
time: 516 us; the launch traced here: 510 us
  waiting for transfers between devices  324 us (63%)
  matrix products  62.4 us (12%)
  local copies, waits for them, and re-layouts  49.8 us (10%)
  starting transfers between devices  32 us (6%)
  blocking collectives  28.8 us (6%)
  other arithmetic  12.2 us (2%)
    all_to_all x1, waiting for transfers between devices, body(): lax.all_to_all(jnp.concatenate([back_real, back_imag], axis=2), 'seq', sp...  92.5 us
    all_to_all x1, waiting for transfers between devices, body(): lax.all_to_all(jnp.concatenate([filter_real, filter_imag], axis=2), 'seq'...  86.9 us
    all_to_all x1, waiting for transfers between devices, body(): lax.all_to_all(jnp.concatenate([signal_real, signal_imag], axis=2), 'seq'...  82.2 us
    dot_general x12, matrix products, along_middle(): jnp.einsum('km,jmx->jkx', matrix, values, precision=lax.Precision.HIGHEST)  39.4 us
    all_to_all x1, waiting for transfers between devices, body(): lax.all_to_all(outgoing, 'dp', split_axis=0, concat_axis=0, tiled=True)  33.4 us
    all_to_all x1, blocking collectives, body(): lax.all_to_all(response, 'seq', split_axis=0, concat_axis=1, tiled=True)  28.8 us
    all_to_all x1, waiting for transfers between devices, body(): lax.all_to_all(signal, 'seq', split_axis=0, concat_axis=0, tiled=True)  23.7 us
    dot_general x10, matrix products, apply_table(): jnp.einsum('ab,brx->arx', matrix, values, precision=lax.Precision.HIGH)  18.1 us
  transfers between devices with their start and end apart: 6, of which 6 were waited for; matrix products, arithmetic and copies ran while one was open for 6% of the time, Pallas kernels for 0%

commit v1 on v0

v1 whole, which is shorter than its diff:
```python
import functools
import math

import jax
import jax.numpy as jnp
import ml_dtypes
import numpy as np
from jax import lax
from jax.experimental import pallas as pl
from jax.experimental.pallas import tpu as pltpu
from jax.sharding import PartitionSpec as P

LANES = 128
FFT_BLOCK = 256
MESH = pl.DeviceIdType.MESH
F32 = jnp.float32
BF16 = jnp.bfloat16


def split_table(table):
    high = table.astype(ml_dtypes.bfloat16)
    low = (table - high.astype(np.float64)).astype(ml_dtypes.bfloat16)
    return high, low


def fourier_tables():
    size = FFT_BLOCK
    freq = np.arange(size)[:, None] * 2 + 1
    angle = math.pi / (2 * size) * (freq * np.arange(size)[None, :] % (4 * size))
    forward = np.concatenate([np.cos(angle), -np.sin(angle)], axis=0)
    places = np.arange(size, 2 * size)[:, None]
    back_angle = math.pi / (2 * size) * (places * freq[:, 0][None, :] % (4 * size))
    inverse = np.concatenate([np.cos(back_angle), -np.sin(back_angle)], axis=1) / size
    return split_table(forward) + split_table(inverse)


def kernel(
    groups, shards, halves, rows, block_len,
    rank_ref, first_ref, q_ref, k_ref, v_ref, f_ref, fwd_hi, fwd_lo, inv_hi, inv_lo,
    out_ref,
    packed, recv, xsend, xbuf, fbuf, rsend, rbuf, xs, spec, fspec, yhi, ylo,
    dp_send, dp_recv, z_send, z_recv,
):
    tokens = q_ref.shape[0]
    blocks = shards * tokens // FFT_BLOCK
    width = halves * LANES
    me_dp = lax.axis_index("dp")
    me_seq = lax.axis_index("seq")
    boundary = first_ref[me_dp]

    barrier = pltpu.get_barrier_semaphore()
    for j in range(1, groups):
        pl.semaphore_signal(
            barrier, inc=1, device_id={"dp": lax.rem(me_dp + j, groups)}, device_id_type=MESH
        )
    for j in range(1, shards):
        pl.semaphore_signal(
            barrier, inc=1, device_id={"seq": lax.rem(me_seq + j, shards)}, device_id_type=MESH
        )

    def lane_tile(index):
        return pl.ds(pl.multiple_of(index * LANES, LANES), LANES)

    def dp_copy(kind, half, j):
        peer = lax.rem(me_dp + j, groups)
        return pltpu.make_async_remote_copy(
            src_ref=packed.at[kind, half, pl.ds(pl.multiple_of(peer * rows, rows), rows)],
            dst_ref=recv.at[kind, half, pl.ds(pl.multiple_of(me_dp * rows, rows), rows)],
            send_sem=dp_send.at[kind, half, j],
            recv_sem=dp_recv.at[kind, half, j],
            device_id={"dp": peer},
            device_id_type=MESH,
        )

    def my_rows():
        return pl.ds(pl.multiple_of(me_seq * tokens, tokens), tokens)

    def z_copy(kind, half, j):
        peer = lax.rem(me_seq + j, shards)
        if kind == 0:
            src = f_ref.at[:, lane_tile(peer * halves + half)]
            dst = fbuf.at[half, my_rows()]
        elif kind == 1:
            src = xsend.at[half, :, lane_tile(peer)]
            dst = xbuf.at[half, my_rows()]
        else:
            src = rsend.at[half, pl.ds(pl.multiple_of(peer * tokens, tokens), tokens)]
            dst = rbuf.at[half, :, lane_tile(me_seq)]
        return pltpu.make_async_remote_copy(
            src_ref=src,
            dst_ref=dst,
            send_sem=z_send.at[kind, half, j],
            recv_sem=z_recv.at[kind, half, j],
            device_id={"seq": peer},
            device_id_type=MESH,
        )

    ranks = rank_ref[...]
    own_rank = rank_ref[pl.ds(me_dp, 1), :]
    own_rank = jnp.broadcast_to(own_rank, ranks.shape)
    group_ids = lax.broadcasted_iota(jnp.int32, ranks.shape, 0)
    earlier_row = lax.broadcasted_iota(jnp.int32, (tokens, tokens), 0)
    earlier_col = lax.broadcasted_iota(jnp.int32, (tokens, tokens), 1)
    earlier = jnp.where(
        (earlier_row // block_len < earlier_col // block_len) & (earlier_row % block_len == 0), 1.0, 0.0
    ).astype(BF16)
    inner = (lax.broadcasted_iota(jnp.int32, ranks.shape, 1) % block_len).astype(F32)
    row_ids = lax.broadcasted_iota(jnp.int32, (rows, tokens), 0).astype(F32)

    def one_hot(mask):
        flags = jnp.where(mask, 1.0, 0.0)
        slots = jnp.dot(flags.astype(BF16), earlier, preferred_element_type=F32)
        target = jnp.where(mask, slots * block_len + inner, -1.0)
        return jnp.concatenate(
            [jnp.where(row_ids == target[p : p + 1], 1.0, 0.0) for p in range(groups)], axis=0
        )

    send_pick = one_hot(ranks == me_dp).astype(BF16)
    recv_pick = jnp.transpose(one_hot(own_rank == group_ids)).astype(BF16)

    def pack(kind, values, tile):
        moved = jnp.dot(send_pick, values, preferred_element_type=F32).astype(BF16)
        for half in range(halves):
            packed[kind, half, :, lane_tile(tile)] = moved[:, half * LANES : (half + 1) * LANES]

    def columns(tile):
        return pl.ds(pl.multiple_of(tile * width, width), width)

    @pl.loop(0, shards)
    def _(tile):
        product = k_ref[:, columns(tile)].astype(F32) * v_ref[:, columns(tile)].astype(F32)
        pack(0, product.astype(BF16), tile)

    pl.semaphore_wait(barrier, groups + shards - 2)
    for half in range(halves):
        for j in range(1, groups):
            dp_copy(0, half, j).start()
    for half in range(halves):
        for j in range(1, shards):
            z_copy(0, half, j).start()

    @pl.loop(0, shards)
    def _(tile):
        pack(1, q_ref[:, columns(tile)], tile)

    for half in range(halves):
        for j in range(1, groups):
            dp_copy(1, half, j).start()
    own = pl.ds(pl.multiple_of(me_dp * rows, rows), rows)
    for half in range(halves):
        for kind in range(2):
            recv[kind, half, own, :] = packed[kind, half, own, :]
        fbuf[half, my_rows(), :] = f_ref[:, lane_tile(me_seq * halves + half)]

    for half in range(halves):
        for j in range(1, groups):
            dp_copy(0, half, j).wait_recv()
        xsend[half] = jnp.dot(recv_pick, recv[0, half], preferred_element_type=F32).astype(BF16)
        for j in range(1, shards):
            z_copy(1, half, j).start()
        xbuf[half, my_rows(), :] = xsend[half, :, lane_tile(me_seq)]

    def forward(values):
        return jnp.dot(fwd_hi[...], values, preferred_element_type=F32) + jnp.dot(
            fwd_lo[...], values, preferred_element_type=F32
        )

    for half in range(halves):
        for j in range(1, shards):
            z_copy(0, half, j).wait_recv()
        for b in range(blocks):
            fspec[half, :, b * LANES : (b + 1) * LANES] = forward(
                fbuf[half, b * FFT_BLOCK : (b + 1) * FFT_BLOCK, :]
            )

    def holds(condition):
        return jnp.where(condition, 1.0, 0.0).astype(F32)

    at_or_after = [holds(FFT_BLOCK * (i + 1) > boundary) for i in range(blocks)]
    before = [1.0 - flag for flag in at_or_after]
    at_block = [
        holds((FFT_BLOCK * i <= boundary) & (FFT_BLOCK * (i + 1) > boundary)) for i in range(blocks)
    ]
    keep = {
        (i, m): jnp.maximum(at_or_after[i], before[m]) for m in range(blocks) for i in range(m)
    }
    place = lax.broadcasted_iota(jnp.int32, (FFT_BLOCK, LANES), 0)
    split = [
        (place + FFT_BLOCK * i < boundary) & (jnp.full(place.shape, FFT_BLOCK * (i + 1)) > boundary)
        for i in range(blocks)
    ]
    extra = blocks * LANES
    step = 16
    sign = jnp.where(lax.broadcasted_iota(jnp.int32, (step, LANES), 0) % 2 == 0, 1.0, -1.0).astype(F32)

    for half in range(halves):
        for j in range(1, shards):
            z_copy(1, half, j).wait_recv()
        early = jnp.zeros((FFT_BLOCK, LANES), F32)
        for i in range(blocks):
            values = xbuf[half, i * FFT_BLOCK : (i + 1) * FFT_BLOCK, :].astype(F32)
            xs[:, i * LANES : (i + 1) * LANES] = jnp.where(split[i], 0.0, values).astype(BF16)
            early = early + jnp.where(split[i] & (place + FFT_BLOCK * i >= 0), values, 0.0) * at_block[i]
        xs[:, extra : extra + LANES] = early.astype(BF16)
        for start in range(0, (blocks + 1) * LANES, 2 * LANES):
            stop = min(start + 2 * LANES, (blocks + 1) * LANES)
            spec[:, start:stop] = forward(xs[:, start:stop])

        @pl.loop(0, FFT_BLOCK // step)
        def _(chunk):
            re = pl.ds(pl.multiple_of(chunk * step, step), step)
            im = pl.ds(pl.multiple_of(FFT_BLOCK + chunk * step, step), step)

            def read(ref, b):
                return ref[re, b * LANES : (b + 1) * LANES], ref[im, b * LANES : (b + 1) * LANES]

            x = [read(spec, b) for b in range(blocks + 1)]
            taps = []
            last = None
            for b in range(blocks):
                a_re, a_im = read(fspec.at[half], b)
                g_re, g_im = sign * a_im, -(sign * a_re)
                if last is not None:
                    g_re, g_im = g_re + last[0], g_im + last[1]
                taps.append((g_re, g_im))
                last = (a_re, a_im)

            def times(a, b):
                return a[0] * b[0] - a[1] * b[1], a[0] * b[1] + a[1] * b[0]

            def put(b, value):
                for part, where in zip(value, (re, im)):
                    high = part.astype(BF16)
                    yhi[where, b * LANES : (b + 1) * LANES] = high
                    ylo[where, b * LANES : (b + 1) * LANES] = (part - high.astype(F32)).astype(BF16)

            edge = times(taps[0], x[blocks])
            for m in range(blocks):
                total = times(taps[0], x[m])
                for i in range(m):
                    term = times(taps[m - i], x[i])
                    total = tuple(t + keep[i, m] * s for t, s in zip(total, term))
                    edge = tuple(t + at_block[m] * s for t, s in zip(edge, term))
                put(m, total)
            put(blocks, edge)

        def inverse(cols):
            return (
                jnp.dot(inv_hi[...], yhi[:, cols], preferred_element_type=F32)
                + jnp.dot(inv_lo[...], yhi[:, cols], preferred_element_type=F32)
                + jnp.dot(inv_hi[...], ylo[:, cols], preferred_element_type=F32)
            )

        edge_time = inverse(slice(extra, extra + LANES))
        for m in range(blocks):
            response = inverse(slice(m * LANES, (m + 1) * LANES))
            rsend[half, m * FFT_BLOCK : (m + 1) * FFT_BLOCK, :] = jnp.where(
                split[m] & (at_block[m] > 0.5), edge_time, response
            ).astype(BF16)
        for j in range(1, shards):
            z_copy(2, half, j).start()
        rbuf[half, :, lane_tile(me_seq)] = rsend[half, my_rows(), :]

    for half in range(halves):
        for j in range(1, groups):
            dp_copy(1, half, j).wait_recv()
    for half in range(halves):
        for j in range(1, shards):
            z_copy(2, half, j).wait_recv()

        @pl.loop(0, shards)
        def _(tile):
            queries = jnp.dot(recv_pick, recv[1, half, :, lane_tile(tile)], preferred_element_type=F32)
            out_ref[:, lane_tile(tile * halves + half)] = (
                queries * rbuf[half, :, lane_tile(tile)].astype(F32)
            ).astype(BF16)

    for half in range(halves):
        for kind in range(2):
            for j in range(1, groups):
                dp_copy(kind, half, j).wait_send()
        for kind in range(3):
            for j in range(1, shards):
                z_copy(kind, half, j).wait_send()


def body(q_arrive, k_arrive, v_arrive, source_rank, first_length, filter_taps):
    groups = lax.axis_size("dp")
    shards = lax.axis_size("seq")
    tokens = q_arrive.shape[1]
    channels = q_arrive.shape[2]
    blocks_here = source_rank.shape[1]
    block_len = tokens // blocks_here
    capacity = max(2, 2 * blocks_here // groups)
    rows = capacity * block_len
    halves = channels // shards // LANES
    blocks = shards * tokens // FFT_BLOCK
    ranks = jnp.repeat(source_rank, block_len, axis=1)
    ranks = jnp.pad(ranks, ((0, -groups % 8), (0, 0)), constant_values=-1)
    tables = [jnp.asarray(table) for table in fourier_tables()]
    vmem = pl.BlockSpec(memory_space=pltpu.VMEM)
    smem = pl.BlockSpec(memory_space=pltpu.SMEM)
    result = pl.pallas_call(
        functools.partial(kernel, groups, shards, halves, rows, block_len),
        out_shape=jax.ShapeDtypeStruct((tokens, channels), BF16),
        in_specs=[vmem, smem] + [vmem] * 8,
        out_specs=vmem,
        scratch_shapes=[
            pltpu.VMEM((2, halves, groups * rows, shards * LANES), BF16),
            pltpu.VMEM((2, halves, groups * rows, shards * LANES), BF16),
            pltpu.VMEM((halves, tokens, shards * LANES), BF16),
            pltpu.VMEM((halves, shards * tokens, LANES), BF16),
            pltpu.VMEM((halves, shards * tokens, LANES), BF16),
            pltpu.VMEM((halves, shards * tokens, LANES), BF16),
            pltpu.VMEM((halves, tokens, shards * LANES), BF16),
            pltpu.VMEM((FFT_BLOCK, (blocks + 1) * LANES), BF16),
            pltpu.VMEM((2 * FFT_BLOCK, (blocks + 1) * LANES), F32),
            pltpu.VMEM((halves, 2 * FFT_BLOCK, blocks * LANES), F32),
            pltpu.VMEM((2 * FFT_BLOCK, (blocks + 1) * LANES), BF16),
            pltpu.VMEM((2 * FFT_BLOCK, (blocks + 1) * LANES), BF16),
            pltpu.SemaphoreType.DMA((2, halves, groups)),
            pltpu.SemaphoreType.DMA((2, halves, groups)),
            pltpu.SemaphoreType.DMA((3, halves, shards)),
            pltpu.SemaphoreType.DMA((3, halves, shards)),
        ],
        compiler_params=pltpu.CompilerParams(
            collective_id=0, has_side_effects=True, vmem_limit_bytes=48 * 1024 * 1024
        ),
    )(ranks, first_length, q_arrive[0], k_arrive[0], v_arrive[0], filter_taps, *tables)
    return result[None]


def solution(mesh):
    return jax.shard_map(
        body,
        mesh=mesh,
        in_specs=(
            P("dp", "seq", None),
            P("dp", "seq", None),
            P("dp", "seq", None),
            P(None, "seq"),
            P(),
            P("seq", None),
        ),
        out_specs=P("dp", "seq", None),
        check_vma=False,
    )
```

time: 516 us -> 54.4 us (0.11)
  the two profiles are of different devices: /device:TPU:1 before, /device:TPU:25 now
where the time goes in v1:
time: 54.4 us; the launch traced here: 54 us
  Pallas kernels  43.6 us (80%)
  local copies, waits for them, and re-layouts  10.3 us (19%)
    pallas_call x1, Pallas kernels, body(): pl.pallas_call(functools.partial(kernel, groups, shards, halves, rows, bl...  43.6 us
    unnamed x21, local copies, waits for them, and re-layouts  10.1 us

profile of v1, /device:TPU:25, one launch (start us, length us, event | category | flops | bytes accessed | tf_op | source)
XLA Modules:
  0.0 54.0 jit_solution(16727231518538993444)
XLA Ops:
  0.0 0.0 copy-start.9
  0.0 0.7 %copy-done.9 = s32[4,32]{1,0:T(4,128)S(1)} copy-done((s32[4,32]{1,0:T(4,128)S(1)}, s32[4,32]{1,0:T(4,128)}, u32[]{:S(2)}) %copy-start.9) | copy-done | bytes 536
  0.7 0.1 broadcast_in_dim.6
  0.8 0.1 reshape.3
  0.9 0.0 copy-start.8
  0.9 0.6 %copy-done.8 = s32[4]{0:T(128)S(1)} copy-done((s32[4]{0:T(128)S(1)}, s32[4]{0:T(128)}, u32[]{:S(2)}) %copy-start.8) | copy-done | bytes 40
  1.5 0.0 copy-start
  1.5 1.0 %copy-done = bf16[1,128,2048]{2,1,0:T(8,128)(2,1)S(1)} copy-done((bf16[1,128,2048]{2,1,0:T(8,128)(2,1)S(1)}, bf16[1,128,2048]{2,1,0:T(8,128)(2,1)}, u32[]{:S(2)}) %copy-start) | copy-done | bytes 524312
  2.6 0.0 copy-start.1
  2.6 1.0 %copy-done.1 = bf16[1,128,2048]{2,1,0:T(8,128)(2,1)S(1)} copy-done((bf16[1,128,2048]{2,1,0:T(8,128)(2,1)S(1)}, bf16[1,128,2048]{2,1,0:T(8,128)(2,1)}, u32[]{:S(2)}) %copy-start.1) | copy-done | bytes 524312
  3.6 0.0 copy-start.2
  3.6 1.0 %copy-done.2 = bf16[1,128,2048]{2,1,0:T(8,128)(2,1)S(1)} copy-done((bf16[1,128,2048]{2,1,0:T(8,128)(2,1)S(1)}, bf16[1,128,2048]{2,1,0:T(8,128)(2,1)}, u32[]{:S(2)}) %copy-start.2) | copy-done | bytes 524312
  4.7 0.0 copy-start.3
  4.7 1.0 %copy-done.3 = bf16[128,2048]{1,0:T(8,128)(2,1)S(1)} copy-done((bf16[128,2048]{1,0:T(8,128)(2,1)S(1)}, bf16[128,2048]{1,0:T(8,128)(2,1)}, u32[]{:S(2)}) %copy-start.3) | copy-done | bytes 524312
  5.7 0.0 copy-start.4
  5.7 0.9 %copy-done.4 = bf16[256,512]{1,0:T(8,128)(2,1)S(1)} copy-done((bf16[256,512]{1,0:T(8,128)(2,1)S(1)}, bf16[256,512]{1,0:T(8,128)(2,1)}, u32[]{:S(2)}) %copy-start.4) | copy-done | bytes 262168
  6.7 0.0 copy-start.5
  6.7 0.9 %copy-done.5 = bf16[256,512]{1,0:T(8,128)(2,1)S(1)} copy-done((bf16[256,512]{1,0:T(8,128)(2,1)S(1)}, bf16[256,512]{1,0:T(8,128)(2,1)}, u32[]{:S(2)}) %copy-start.5) | copy-done | bytes 262168
  7.6 0.0 copy-start.6
  7.6 0.9 %copy-done.6 = bf16[512,256]{1,0:T(8,128)(2,1)S(1)} copy-done((bf16[512,256]{1,0:T(8,128)(2,1)S(1)}, bf16[512,256]{1,0:T(8,128)(2,1)}, u32[]{:S(2)}) %copy-start.6) | copy-done | bytes 262168
  8.6 0.0 copy-start.7
  8.6 0.9 %copy-done.7 = bf16[512,256]{1,0:T(8,128)(2,1)S(1)} copy-done((bf16[512,256]{1,0:T(8,128)(2,1)S(1)}, bf16[512,256]{1,0:T(8,128)(2,1)}, u32[]{:S(2)}) %copy-start.7) | copy-done | bytes 262168
  9.5 43.6 %shard_map.100 = bf16[128,2048]{1,0:T(8,128)(2,1)S(1)} custom-call(s32[8,128]{1,0:T(8,128)S(1)} %pad.4.rank_ref, s32[4]{0:T(128)S(1)} %copy-done.8, bf16[128,2048]{1,0:T(8,128)(2,1)S(1)} %bitcast.5, bf16[128,2048]{1,0:T(8,128)(2,1)S(1)} %bitcast.6, bf16[128,2048]{1,0:T(8,128)(2,1)S(1)} %bitcast.7, bf16[128,2048]{1,0:T(8,128)(2,1)S(1)} %copy-done.3, ...), custom_call_target="tpu_custom_call" | custom-call | tf_op jit(solution)/shard_map/pallas_call | solution.py:303
  53.2 0.8 %copy.12 = bf16[1,128,2048]{2,1,0:T(8,128)(2,1)} copy(bf16[1,128,2048]{2,1,0:T(8,128)(2,1)S(1)} %bitcast.4) | data formatting | bytes 1048576
  (1 shorter events, 0.0 us)
Async XLA Ops:
  0.0 0.7 %copy-start.9 = (s32[4,32]{1,0:T(4,128)S(1)}, s32[4,32]{1,0:T(4,128)}, u32[]{:S(2)}) copy-start(s32[4,32]{1,0:T(4,128)} %param.13) | copy-start | bytes 1540
  0.9 0.7 %copy-start.8 = (s32[4]{0:T(128)S(1)}, s32[4]{0:T(128)}, u32[]{:S(2)}) copy-start(s32[4]{0:T(128)} %first_ref.1) | copy-start | bytes 52
  1.5 1.0 %copy-start = (bf16[1,128,2048]{2,1,0:T(8,128)(2,1)S(1)}, bf16[1,128,2048]{2,1,0:T(8,128)(2,1)}, u32[]{:S(2)}) copy-start(bf16[1,128,2048]{2,1,0:T(8,128)(2,1)} %param.10) | copy-start | bytes 1572868
  2.6 1.0 %copy-start.1 = (bf16[1,128,2048]{2,1,0:T(8,128)(2,1)S(1)}, bf16[1,128,2048]{2,1,0:T(8,128)(2,1)}, u32[]{:S(2)}) copy-start(bf16[1,128,2048]{2,1,0:T(8,128)(2,1)} %param.11) | copy-start | bytes 1572868
  3.6 1.0 %copy-start.2 = (bf16[1,128,2048]{2,1,0:T(8,128)(2,1)S(1)}, bf16[1,128,2048]{2,1,0:T(8,128)(2,1)}, u32[]{:S(2)}) copy-start(bf16[1,128,2048]{2,1,0:T(8,128)(2,1)} %param.12) | copy-start | bytes 1572868
  4.7 1.0 %copy-start.3 = (bf16[128,2048]{1,0:T(8,128)(2,1)S(1)}, bf16[128,2048]{1,0:T(8,128)(2,1)}, u32[]{:S(2)}) copy-start(bf16[128,2048]{1,0:T(8,128)(2,1)} %f_ref.1) | copy-start | bytes 1572868
  5.7 0.9 %copy-start.4 = (bf16[256,512]{1,0:T(8,128)(2,1)S(1)}, bf16[256,512]{1,0:T(8,128)(2,1)}, u32[]{:S(2)}) copy-start(bf16[256,512]{1,0:T(8,128)(2,1)} %constant.13.clone.inv_lo) | copy-start | bytes 786436
  6.7 0.9 %copy-start.5 = (bf16[256,512]{1,0:T(8,128)(2,1)S(1)}, bf16[256,512]{1,0:T(8,128)(2,1)}, u32[]{:S(2)}) copy-start(bf16[256,512]{1,0:T(8,128)(2,1)} %constant.12.clone.inv_hi) | copy-start | bytes 786436
  7.6 0.9 %copy-start.6 = (bf16[512,256]{1,0:T(8,128)(2,1)S(1)}, bf16[512,256]{1,0:T(8,128)(2,1)}, u32[]{:S(2)}) copy-start(bf16[512,256]{1,0:T(8,128)(2,1)} %constant.11.clone.fwd_lo) | copy-start | bytes 786436
  8.6 0.9 %copy-start.7 = (bf16[512,256]{1,0:T(8,128)(2,1)S(1)}, bf16[512,256]{1,0:T(8,128)(2,1)}, u32[]{:S(2)}) copy-start(bf16[512,256]{1,0:T(8,128)(2,1)} %constant.10.clone.fwd_hi) | copy-start | bytes 786436

commit v2 on v1

--- a/solution.py
+++ b/solution.py
@@ -12,6 +12,7 @@
 
 LANES = 128
 FFT_BLOCK = 256
+FILTER_PARTS = 4
 MESH = pl.DeviceIdType.MESH
 F32 = jnp.float32
 BF16 = jnp.bfloat16
@@ -36,12 +37,14 @@
 
 def kernel(
     groups, shards, halves, rows, block_len,
-    rank_ref, first_ref, q_ref, k_ref, v_ref, f_ref, fwd_hi, fwd_lo, inv_hi, inv_lo,
+    rank_ref, first_ref, q_hbm, k_hbm, v_hbm, f_hbm, fwd_hi_hbm, fwd_lo_hbm, inv_hi_hbm, inv_lo_hbm,
     out_ref,
-    packed, recv, xsend, xbuf, fbuf, rsend, rbuf, xs, spec, fspec, yhi, ylo,
-    dp_send, dp_recv, z_send, z_recv,
+    q_ref, k_ref, v_ref, f_ref, fwd_hi, fwd_lo, inv_hi, inv_lo,
+    packed, recv, xsend, xbuf, fbuf, rsend, rbuf, qbuf, xs, spec, fspec, yhi, ylo,
+    load_sem, dp_send, dp_recv, f_send, f_recv, z_send, z_recv,
 ):
     tokens = q_ref.shape[0]
+    part_rows = tokens // FILTER_PARTS
     blocks = shards * tokens // FFT_BLOCK
     width = halves * LANES
     me_dp = lax.axis_index("dp")
@@ -57,6 +60,24 @@
         pl.semaphore_signal(
             barrier, inc=1, device_id={"seq": lax.rem(me_seq + j, shards)}, device_id_type=MESH
         )
+
+    loads = [
+        pltpu.make_async_copy(src, dst, load_sem.at[n])
+        for n, (src, dst) in enumerate(
+            [
+                (k_hbm, k_ref),
+                (v_hbm, v_ref),
+                (f_hbm, f_ref),
+                (q_hbm, q_ref),
+                (fwd_hi_hbm, fwd_hi),
+                (fwd_lo_hbm, fwd_lo),
+                (inv_hi_hbm, inv_hi),
+                (inv_lo_hbm, inv_lo),
+            ]
+        )
+    ]
+    for load in loads:
+        load.start()
 
     def lane_tile(index):
         return pl.ds(pl.multiple_of(index * LANES, LANES), LANES)
@@ -72,14 +93,30 @@
             device_id_type=MESH,
         )
 
+    my_part = lax.rem(me_dp, FILTER_PARTS)
+
+    def part_slice(index):
+        return pl.ds(pl.multiple_of(index * part_rows, part_rows), part_rows)
+
+    def f_copy(half, j):
+        peer = me_dp - my_part + lax.rem(my_part + j, FILTER_PARTS)
+        return pltpu.make_async_remote_copy(
+            src_ref=fbuf.at[half, my_part],
+            dst_ref=fbuf.at[half, my_part],
+            send_sem=f_send.at[half, j],
+            recv_sem=f_recv.at[half, j],
+            device_id={"dp": peer},
+            device_id_type=MESH,
+        )
+
     def my_rows():
         return pl.ds(pl.multiple_of(me_seq * tokens, tokens), tokens)
 
     def z_copy(kind, half, j):
         peer = lax.rem(me_seq + j, shards)
         if kind == 0:
-            src = f_ref.at[:, lane_tile(peer * halves + half)]
-            dst = fbuf.at[half, my_rows()]
+            src = f_ref.at[part_slice(my_part), lane_tile(peer * halves + half)]
+            dst = fbuf.at[half, my_part, part_slice(me_seq)]
         elif kind == 1:
             src = xsend.at[half, :, lane_tile(peer)]
             dst = xbuf.at[half, my_rows()]
@@ -118,39 +155,51 @@
     send_pick = one_hot(ranks == me_dp).astype(BF16)
     recv_pick = jnp.transpose(one_hot(own_rank == group_ids)).astype(BF16)
 
-    def pack(kind, values, tile):
+    def pack(kind, half, tile, read):
+        values = jnp.concatenate([read(tile * 2), read(tile * 2 + 1)], axis=1)
         moved = jnp.dot(send_pick, values, preferred_element_type=F32).astype(BF16)
-        for half in range(halves):
-            packed[kind, half, :, lane_tile(tile)] = moved[:, half * LANES : (half + 1) * LANES]
-
-    def columns(tile):
-        return pl.ds(pl.multiple_of(tile * width, width), width)
-
-    @pl.loop(0, shards)
-    def _(tile):
-        product = k_ref[:, columns(tile)].astype(F32) * v_ref[:, columns(tile)].astype(F32)
-        pack(0, product.astype(BF16), tile)
+        where = pl.ds(pl.multiple_of(tile * 2 * LANES, 2 * LANES), 2 * LANES)
+        packed[kind, half, :, where] = moved
 
     pl.semaphore_wait(barrier, groups + shards - 2)
-    for half in range(halves):
+    loads[2].wait()
+    for half in range(halves):
+        for j in range(1, shards):
+            z_copy(0, half, j).start()
+    loads[0].wait()
+    loads[1].wait()
+    for half in range(halves):
+
+        def product(tile):
+            cols = lane_tile(tile * halves + half)
+            return (k_ref[:, cols].astype(F32) * v_ref[:, cols].astype(F32)).astype(BF16)
+
+        @pl.loop(0, shards // 2)
+        def _(tile):
+            pack(0, half, tile, product)
+
         for j in range(1, groups):
             dp_copy(0, half, j).start()
-    for half in range(halves):
-        for j in range(1, shards):
-            z_copy(0, half, j).start()
-
-    @pl.loop(0, shards)
-    def _(tile):
-        pack(1, q_ref[:, columns(tile)], tile)
-
-    for half in range(halves):
-        for j in range(1, groups):
-            dp_copy(1, half, j).start()
+
+    loads[3].wait()
+    for half in range(halves):
+
+        @pl.loop(0, shards // 2)
+        def _(tile):
+            pack(1, half, tile, lambda t: q_ref[:, lane_tile(t * halves + half)])
+
     own = pl.ds(pl.multiple_of(me_dp * rows, rows), rows)
     for half in range(halves):
         for kind in range(2):
             recv[kind, half, own, :] = packed[kind, half, own, :]
-        fbuf[half, my_rows(), :] = f_ref[:, lane_tile(me_seq * halves + half)]
+        fbuf[half, my_part, part_slice(me_seq), :] = f_ref[
+            part_slice(my_part), lane_tile(me_seq * halves + half)
+        ]
+    for half in range(halves):
+        for j in range(1, shards):
+            z_copy(0, half, j).wait_recv()
+        for j in range(1, FILTER_PARTS):
+            f_copy(half, j).start()
 
     for half in range(halves):
         for j in range(1, groups):
@@ -159,6 +208,11 @@
         for j in range(1, shards):
             z_copy(1, half, j).start()
         xbuf[half, my_rows(), :] = xsend[half, :, lane_tile(me_seq)]
+    for half in range(halves):
+        for j in range(1, groups):
+            dp_copy(1, half, j).start()
+    for load in loads[4:]:
+        load.wait()
 
     def forward(values):
         return jnp.dot(fwd_hi[...], values, preferred_element_type=F32) + jnp.dot(
@@ -166,11 +220,23 @@
         )
 
     for half in range(halves):
-        for j in range(1, shards):
-            z_copy(0, half, j).wait_recv()
-        for b in range(blocks):
-            fspec[half, :, b * LANES : (b + 1) * LANES] = forward(
-                fbuf[half, b * FFT_BLOCK : (b + 1) * FFT_BLOCK, :]
+        for j in range(1, FILTER_PARTS):
+            f_copy(half, j).wait_recv()
+
+        def filter_block(b):
+            ranges = range(b * FFT_BLOCK // tokens, (b + 1) * FFT_BLOCK // tokens)
+            return jnp.concatenate(
+                [
+                    fbuf[half, part, r * part_rows : (r + 1) * part_rows, :]
+                    for r in ranges
+                    for part in range(FILTER_PARTS)
+                ],
+                axis=0,
+            )
+
+        for b in range(0, blocks, 2):
+            fspec[half, :, b * LANES : (b + 2) * LANES] = forward(
+                jnp.concatenate([filter_block(b), filter_block(b + 1)], axis=1)
             )
 
     def holds(condition):
@@ -200,7 +266,7 @@
         for i in range(blocks):
             values = xbuf[half, i * FFT_BLOCK : (i + 1) * FFT_BLOCK, :].astype(F32)
             xs[:, i * LANES : (i + 1) * LANES] = jnp.where(split[i], 0.0, values).astype(BF16)
-            early = early + jnp.where(split[i] & (place + FFT_BLOCK * i >= 0), values, 0.0) * at_block[i]
+            early = early + jnp.where(split[i], values, 0.0) * at_block[i]
         xs[:, extra : extra + LANES] = early.astype(BF16)
         for start in range(0, (blocks + 1) * LANES, 2 * LANES):
             stop = min(start + 2 * LANES, (blocks + 1) * LANES)
@@ -252,11 +318,14 @@
             )
 
         edge_time = inverse(slice(extra, extra + LANES))
-        for m in range(blocks):
-            response = inverse(slice(m * LANES, (m + 1) * LANES))
-            rsend[half, m * FFT_BLOCK : (m + 1) * FFT_BLOCK, :] = jnp.where(
-                split[m] & (at_block[m] > 0.5), edge_time, response
-            ).astype(BF16)
+        for start in range(0, blocks, 2):
+            response = inverse(slice(start * LANES, (start + 2) * LANES))
+            for m in (start, start + 1):
+                rsend[half, m * FFT_BLOCK : (m + 1) * FFT_BLOCK, :] = jnp.where(
+                    split[m] & (at_block[m] > 0.5),
+                    edge_time,
+                    response[:, (m - start) * LANES : (m - start + 1) * LANES],
+                ).astype(BF16)
         for j in range(1, shards):
             z_copy(2, half, j).start()
         rbuf[half, :, lane_tile(me_seq)] = rsend[half, my_rows(), :]
@@ -264,21 +333,23 @@
     for half in range(halves):
         for j in range(1, groups):
             dp_copy(1, half, j).wait_recv()
+        qbuf[half] = jnp.dot(recv_pick, recv[1, half], preferred_element_type=F32).astype(BF16)
     for half in range(halves):
         for j in range(1, shards):
             z_copy(2, half, j).wait_recv()
-
-        @pl.loop(0, shards)
-        def _(tile):
-            queries = jnp.dot(recv_pick, recv[1, half, :, lane_tile(tile)], preferred_element_type=F32)
-            out_ref[:, lane_tile(tile * halves + half)] = (
-                queries * rbuf[half, :, lane_tile(tile)].astype(F32)
+        for tile in range(shards):
+            cols = slice(tile * LANES, (tile + 1) * LANES)
+            first = (tile * halves + half) * LANES
+            out_ref[:, first : first + LANES] = (
+                qbuf[half, :, cols].astype(F32) * rbuf[half, :, cols].astype(F32)
             ).astype(BF16)
 
     for half in range(halves):
         for kind in range(2):
             for j in range(1, groups):
                 dp_copy(kind, half, j).wait_send()
+        for j in range(1, FILTER_PARTS):
+            f_copy(half, j).wait_send()
         for kind in range(3):
             for j in range(1, shards):
                 z_copy(kind, half, j).wait_send()
@@ -300,26 +371,33 @@
     tables = [jnp.asarray(table) for table in fourier_tables()]
     vmem = pl.BlockSpec(memory_space=pltpu.VMEM)
     smem = pl.BlockSpec(memory_space=pltpu.SMEM)
+    hbm = pl.BlockSpec(memory_space=pltpu.HBM)
+    local = pltpu.VMEM((tokens, channels), BF16)
+    table_scratch = [pltpu.VMEM(table.shape, BF16) for table in tables]
     result = pl.pallas_call(
         functools.partial(kernel, groups, shards, halves, rows, block_len),
         out_shape=jax.ShapeDtypeStruct((tokens, channels), BF16),
-        in_specs=[vmem, smem] + [vmem] * 8,
+        in_specs=[vmem, smem] + [hbm] * 8,
         out_specs=vmem,
-        scratch_shapes=[
+        scratch_shapes=[local] * 4 + table_scratch + [
             pltpu.VMEM((2, halves, groups * rows, shards * LANES), BF16),
             pltpu.VMEM((2, halves, groups * rows, shards * LANES), BF16),
             pltpu.VMEM((halves, tokens, shards * LANES), BF16),
             pltpu.VMEM((halves, shards * tokens, LANES), BF16),
+            pltpu.VMEM((halves, FILTER_PARTS, shards * tokens // FILTER_PARTS, LANES), BF16),
             pltpu.VMEM((halves, shards * tokens, LANES), BF16),
-            pltpu.VMEM((halves, shards * tokens, LANES), BF16),
+            pltpu.VMEM((halves, tokens, shards * LANES), BF16),
             pltpu.VMEM((halves, tokens, shards * LANES), BF16),
             pltpu.VMEM((FFT_BLOCK, (blocks + 1) * LANES), BF16),
             pltpu.VMEM((2 * FFT_BLOCK, (blocks + 1) * LANES), F32),
             pltpu.VMEM((halves, 2 * FFT_BLOCK, blocks * LANES), F32),
             pltpu.VMEM((2 * FFT_BLOCK, (blocks + 1) * LANES), BF16),
             pltpu.VMEM((2 * FFT_BLOCK, (blocks + 1) * LANES), BF16),
+            pltpu.SemaphoreType.DMA((8,)),
             pltpu.SemaphoreType.DMA((2, halves, groups)),
             pltpu.SemaphoreType.DMA((2, halves, groups)),
+            pltpu.SemaphoreType.DMA((halves, FILTER_PARTS)),
+            pltpu.SemaphoreType.DMA((halves, FILTER_PARTS)),
             pltpu.SemaphoreType.DMA((3, halves, shards)),
             pltpu.SemaphoreType.DMA((3, halves, shards)),
         ],

time: 54.4 us -> 51.7 us (0.950)
  the two profiles are of different devices: /device:TPU:25 before, /device:TPU:1 now
where the time goes in v2:
time: 51.7 us; the launch traced here: 51.3 us
  Pallas kernels  41 us (79%)
  local copies, waits for them, and re-layouts  10.3 us (20%)
    pallas_call x1, Pallas kernels, body(): pl.pallas_call(functools.partial(kernel, groups, shards, halves, rows, bl...  41 us
    unnamed x21, local copies, waits for them, and re-layouts  10.1 us

profile of v2, /device:TPU:1, one launch (start us, length us, event | category | flops | bytes accessed | tf_op | source)
XLA Modules:
  0.0 51.3 jit_solution(11834843531165963818)
XLA Ops:
  0.0 0.0 copy-start.9
  0.0 0.7 %copy-done.9 = s32[4,32]{1,0:T(4,128)S(1)} copy-done((s32[4,32]{1,0:T(4,128)S(1)}, s32[4,32]{1,0:T(4,128)}, u32[]{:S(2)}) %copy-start.9) | copy-done | bytes 536
  0.7 0.1 broadcast_in_dim.6
  0.8 0.1 reshape.3
  0.9 0.0 copy-start.8
  0.9 0.6 %copy-done.8 = s32[4]{0:T(128)S(1)} copy-done((s32[4]{0:T(128)S(1)}, s32[4]{0:T(128)}, u32[]{:S(2)}) %copy-start.8) | copy-done | bytes 40
  1.5 0.0 copy-start
  1.5 1.0 %copy-done = bf16[1,128,2048]{2,1,0:T(8,128)(2,1)S(1)} copy-done((bf16[1,128,2048]{2,1,0:T(8,128)(2,1)S(1)}, bf16[1,128,2048]{2,1,0:T(8,128)(2,1)}, u32[]{:S(2)}) %copy-start) | copy-done | bytes 524312
  2.6 0.0 copy-start.1
  2.6 1.0 %copy-done.1 = bf16[1,128,2048]{2,1,0:T(8,128)(2,1)S(1)} copy-done((bf16[1,128,2048]{2,1,0:T(8,128)(2,1)S(1)}, bf16[1,128,2048]{2,1,0:T(8,128)(2,1)}, u32[]{:S(2)}) %copy-start.1) | copy-done | bytes 524312
  3.6 0.0 copy-start.2
  3.6 1.0 %copy-done.2 = bf16[1,128,2048]{2,1,0:T(8,128)(2,1)S(1)} copy-done((bf16[1,128,2048]{2,1,0:T(8,128)(2,1)S(1)}, bf16[1,128,2048]{2,1,0:T(8,128)(2,1)}, u32[]{:S(2)}) %copy-start.2) | copy-done | bytes 524312
  4.7 0.0 copy-start.3
  4.7 1.0 %copy-done.3 = bf16[128,2048]{1,0:T(8,128)(2,1)S(1)} copy-done((bf16[128,2048]{1,0:T(8,128)(2,1)S(1)}, bf16[128,2048]{1,0:T(8,128)(2,1)}, u32[]{:S(2)}) %copy-start.3) | copy-done | bytes 524312
  5.7 0.0 copy-start.4
  5.7 0.9 %copy-done.4 = bf16[256,512]{1,0:T(8,128)(2,1)S(1)} copy-done((bf16[256,512]{1,0:T(8,128)(2,1)S(1)}, bf16[256,512]{1,0:T(8,128)(2,1)}, u32[]{:S(2)}) %copy-start.4) | copy-done | bytes 262168
  6.7 0.0 copy-start.5
  6.7 0.9 %copy-done.5 = bf16[256,512]{1,0:T(8,128)(2,1)S(1)} copy-done((bf16[256,512]{1,0:T(8,128)(2,1)S(1)}, bf16[256,512]{1,0:T(8,128)(2,1)}, u32[]{:S(2)}) %copy-start.5) | copy-done | bytes 262168
  7.6 0.0 copy-start.6
  7.6 0.9 %copy-done.6 = bf16[512,256]{1,0:T(8,128)(2,1)S(1)} copy-done((bf16[512,256]{1,0:T(8,128)(2,1)S(1)}, bf16[512,256]{1,0:T(8,128)(2,1)}, u32[]{:S(2)}) %copy-start.6) | copy-done | bytes 262168
  8.6 0.0 copy-start.7
  8.6 0.9 %copy-done.7 = bf16[512,256]{1,0:T(8,128)(2,1)S(1)} copy-done((bf16[512,256]{1,0:T(8,128)(2,1)S(1)}, bf16[512,256]{1,0:T(8,128)(2,1)}, u32[]{:S(2)}) %copy-start.7) | copy-done | bytes 262168
  9.5 41.0 %shard_map.100 = bf16[128,2048]{1,0:T(8,128)(2,1)S(1)} custom-call(s32[8,128]{1,0:T(8,128)S(1)} %pad.4.rank_ref, s32[4]{0:T(128)S(1)} %copy-done.8, bf16[128,2048]{1,0:T(8,128)(2,1)S(1)} %bitcast.5, bf16[128,2048]{1,0:T(8,128)(2,1)S(1)} %bitcast.6, bf16[128,2048]{1,0:T(8,128)(2,1)S(1)} %bitcast.7, bf16[128,2048]{1,0:T(8,128)(2,1)S(1)} %copy-done.3, ...), custom_call_target="tpu_custom_call" | custom-call | tf_op jit(solution)/shard_map/pallas_call | solution.py:377
  50.5 0.8 %copy.12 = bf16[1,128,2048]{2,1,0:T(8,128)(2,1)} copy(bf16[1,128,2048]{2,1,0:T(8,128)(2,1)S(1)} %bitcast.4) | data formatting | bytes 1048576
  (1 shorter events, 0.0 us)
Async XLA Ops:
  0.0 0.7 %copy-start.9 = (s32[4,32]{1,0:T(4,128)S(1)}, s32[4,32]{1,0:T(4,128)}, u32[]{:S(2)}) copy-start(s32[4,32]{1,0:T(4,128)} %param.13) | copy-start | bytes 1540
  0.9 0.7 %copy-start.8 = (s32[4]{0:T(128)S(1)}, s32[4]{0:T(128)}, u32[]{:S(2)}) copy-start(s32[4]{0:T(128)} %first_ref.1) | copy-start | bytes 52
  1.5 1.0 %copy-start = (bf16[1,128,2048]{2,1,0:T(8,128)(2,1)S(1)}, bf16[1,128,2048]{2,1,0:T(8,128)(2,1)}, u32[]{:S(2)}) copy-start(bf16[1,128,2048]{2,1,0:T(8,128)(2,1)} %param.10) | copy-start | bytes 1572868
  2.6 1.0 %copy-start.1 = (bf16[1,128,2048]{2,1,0:T(8,128)(2,1)S(1)}, bf16[1,128,2048]{2,1,0:T(8,128)(2,1)}, u32[]{:S(2)}) copy-start(bf16[1,128,2048]{2,1,0:T(8,128)(2,1)} %param.11) | copy-start | bytes 1572868
  3.6 1.0 %copy-start.2 = (bf16[1,128,2048]{2,1,0:T(8,128)(2,1)S(1)}, bf16[1,128,2048]{2,1,0:T(8,128)(2,1)}, u32[]{:S(2)}) copy-start(bf16[1,128,2048]{2,1,0:T(8,128)(2,1)} %param.12) | copy-start | bytes 1572868
  4.7 1.0 %copy-start.3 = (bf16[128,2048]{1,0:T(8,128)(2,1)S(1)}, bf16[128,2048]{1,0:T(8,128)(2,1)}, u32[]{:S(2)}) copy-start(bf16[128,2048]{1,0:T(8,128)(2,1)} %f_hbm.1) | copy-start | bytes 1572868
  5.7 0.9 %copy-start.4 = (bf16[256,512]{1,0:T(8,128)(2,1)S(1)}, bf16[256,512]{1,0:T(8,128)(2,1)}, u32[]{:S(2)}) copy-start(bf16[256,512]{1,0:T(8,128)(2,1)} %constant.13.clone.inv_lo_hbm) | copy-start | bytes 786436
  6.7 0.9 %copy-start.5 = (bf16[256,512]{1,0:T(8,128)(2,1)S(1)}, bf16[256,512]{1,0:T(8,128)(2,1)}, u32[]{:S(2)}) copy-start(bf16[256,512]{1,0:T(8,128)(2,1)} %constant.12.clone.inv_hi_hbm) | copy-start | bytes 786436
  7.6 0.9 %copy-start.6 = (bf16[512,256]{1,0:T(8,128)(2,1)S(1)}, bf16[512,256]{1,0:T(8,128)(2,1)}, u32[]{:S(2)}) copy-start(bf16[512,256]{1,0:T(8,128)(2,1)} %constant.11.clone.fwd_lo_hbm) | copy-start | bytes 786436
  8.6 0.9 %copy-start.7 = (bf16[512,256]{1,0:T(8,128)(2,1)S(1)}, bf16[512,256]{1,0:T(8,128)(2,1)}, u32[]{:S(2)}) copy-start(bf16[512,256]{1,0:T(8,128)(2,1)} %constant.10.clone.fwd_hi_hbm) | copy-start | bytes 786436

commit v3 on v2

--- a/solution.py
+++ b/solution.py
@@ -31,25 +31,23 @@
     forward = np.concatenate([np.cos(angle), -np.sin(angle)], axis=0)
     places = np.arange(size, 2 * size)[:, None]
     back_angle = math.pi / (2 * size) * (places * freq[:, 0][None, :] % (4 * size))
-    inverse = np.concatenate([np.cos(back_angle), -np.sin(back_angle)], axis=1) / size
-    return split_table(forward) + split_table(inverse)
+    inverse = np.concatenate([np.cos(back_angle), -np.sin(back_angle)], axis=0) / size
+    return np.stack(split_table(forward) + split_table(inverse))
 
 
 def kernel(
     groups, shards, halves, rows, block_len,
-    rank_ref, first_ref, q_hbm, k_hbm, v_hbm, f_hbm, fwd_hi_hbm, fwd_lo_hbm, inv_hi_hbm, inv_lo_hbm,
+    rank_hbm, first_hbm, q_hbm, k_hbm, v_hbm, f_hbm, tables_hbm,
     out_ref,
-    q_ref, k_ref, v_ref, f_ref, fwd_hi, fwd_lo, inv_hi, inv_lo,
+    rank_ref, first_ref, q_ref, k_ref, v_ref, f_ref, tables,
     packed, recv, xsend, xbuf, fbuf, rsend, rbuf, qbuf, xs, spec, fspec, yhi, ylo,
     load_sem, dp_send, dp_recv, f_send, f_recv, z_send, z_recv,
 ):
     tokens = q_ref.shape[0]
     part_rows = tokens // FILTER_PARTS
     blocks = shards * tokens // FFT_BLOCK
-    width = halves * LANES
     me_dp = lax.axis_index("dp")
     me_seq = lax.axis_index("seq")
-    boundary = first_ref[me_dp]
 
     barrier = pltpu.get_barrier_semaphore()
     for j in range(1, groups):
@@ -69,14 +67,13 @@
                 (v_hbm, v_ref),
                 (f_hbm, f_ref),
                 (q_hbm, q_ref),
-                (fwd_hi_hbm, fwd_hi),
-                (fwd_lo_hbm, fwd_lo),
-                (inv_hi_hbm, inv_hi),
-                (inv_lo_hbm, inv_lo),
+                (tables_hbm, tables),
+                (rank_hbm, rank_ref),
+                (first_hbm, first_ref),
             ]
         )
     ]
-    for load in loads:
+    for load in [loads[5], loads[6], *loads[:5]]:
         load.start()
 
     def lane_tile(index):
@@ -132,10 +129,14 @@
             device_id_type=MESH,
         )
 
-    ranks = rank_ref[...]
-    own_rank = rank_ref[pl.ds(me_dp, 1), :]
+    loads[-2].wait()
+    widen_row = lax.broadcasted_iota(jnp.int32, (tokens // block_len, tokens), 0)
+    widen_col = lax.broadcasted_iota(jnp.int32, (tokens // block_len, tokens), 1)
+    widen = jnp.where(widen_col // block_len == widen_row, 1.0, 0.0).astype(BF16)
+    ranks = jnp.dot(rank_ref[...].astype(F32).astype(BF16), widen, preferred_element_type=F32)
+    group_ids = lax.broadcasted_iota(jnp.int32, ranks.shape, 0)
+    own_rank = jnp.sum(jnp.where(group_ids == me_dp, ranks, 0.0), axis=0, keepdims=True)
     own_rank = jnp.broadcast_to(own_rank, ranks.shape)
-    group_ids = lax.broadcasted_iota(jnp.int32, ranks.shape, 0)
     earlier_row = lax.broadcasted_iota(jnp.int32, (tokens, tokens), 0)
     earlier_col = lax.broadcasted_iota(jnp.int32, (tokens, tokens), 1)
     earlier = jnp.where(
@@ -152,8 +153,8 @@
             [jnp.where(row_ids == target[p : p + 1], 1.0, 0.0) for p in range(groups)], axis=0
         )
 
-    send_pick = one_hot(ranks == me_dp).astype(BF16)
-    recv_pick = jnp.transpose(one_hot(own_rank == group_ids)).astype(BF16)
+    send_pick = one_hot(ranks == me_dp.astype(F32)).astype(BF16)
+    recv_pick = jnp.transpose(one_hot(own_rank == group_ids.astype(F32))).astype(BF16)
 
     def pack(kind, half, tile, read):
         values = jnp.concatenate([read(tile * 2), read(tile * 2 + 1)], axis=1)
@@ -211,12 +212,13 @@
     for half in range(halves):
         for j in range(1, groups):
             dp_copy(1, half, j).start()
-    for load in loads[4:]:
+    for load in [loads[4], loads[6]]:
         load.wait()
+    boundary = first_ref[me_dp]
 
     def forward(values):
-        return jnp.dot(fwd_hi[...], values, preferred_element_type=F32) + jnp.dot(
-            fwd_lo[...], values, preferred_element_type=F32
+        return jnp.dot(tables[0], values, preferred_element_type=F32) + jnp.dot(
+            tables[1], values, preferred_element_type=F32
         )
 
     for half in range(halves):
@@ -310,11 +312,16 @@
                 put(m, total)
             put(blocks, edge)
 
+        def back(table, values):
+            return jnp.dot(table[:FFT_BLOCK], values[:FFT_BLOCK], preferred_element_type=F32) + jnp.dot(
+                table[FFT_BLOCK:], values[FFT_BLOCK:], preferred_element_type=F32
+            )
+
         def inverse(cols):
             return (
-                jnp.dot(inv_hi[...], yhi[:, cols], preferred_element_type=F32)
-                + jnp.dot(inv_lo[...], yhi[:, cols], preferred_element_type=F32)
-                + jnp.dot(inv_hi[...], ylo[:, cols], preferred_element_type=F32)
+                back(tables[2], yhi[:, cols])
+                + back(tables[3], yhi[:, cols])
+                + back(tables[2], ylo[:, cols])
             )
 
         edge_time = inverse(slice(extra, extra + LANES))
@@ -366,20 +373,19 @@
     rows = capacity * block_len
     halves = channels // shards // LANES
     blocks = shards * tokens // FFT_BLOCK
-    ranks = jnp.repeat(source_rank, block_len, axis=1)
-    ranks = jnp.pad(ranks, ((0, -groups % 8), (0, 0)), constant_values=-1)
-    tables = [jnp.asarray(table) for table in fourier_tables()]
+    tables = jnp.asarray(fourier_tables())
     vmem = pl.BlockSpec(memory_space=pltpu.VMEM)
-    smem = pl.BlockSpec(memory_space=pltpu.SMEM)
     hbm = pl.BlockSpec(memory_space=pltpu.HBM)
     local = pltpu.VMEM((tokens, channels), BF16)
-    table_scratch = [pltpu.VMEM(table.shape, BF16) for table in tables]
     result = pl.pallas_call(
         functools.partial(kernel, groups, shards, halves, rows, block_len),
         out_shape=jax.ShapeDtypeStruct((tokens, channels), BF16),
-        in_specs=[vmem, smem] + [hbm] * 8,
+        in_specs=[hbm] * 7,
         out_specs=vmem,
-        scratch_shapes=[local] * 4 + table_scratch + [
+        scratch_shapes=[
+            pltpu.VMEM(source_rank.shape, jnp.int32),
+            pltpu.SMEM(first_length.shape, jnp.int32),
+        ] + [local] * 4 + [pltpu.VMEM(tables.shape, BF16)] + [
             pltpu.VMEM((2, halves, groups * rows, shards * LANES), BF16),
             pltpu.VMEM((2, halves, groups * rows, shards * LANES), BF16),
             pltpu.VMEM((halves, tokens, shards * LANES), BF16),
@@ -393,7 +399,7 @@
             pltpu.VMEM((halves, 2 * FFT_BLOCK, blocks * LANES), F32),
             pltpu.VMEM((2 * FFT_BLOCK, (blocks + 1) * LANES), BF16),
             pltpu.VMEM((2 * FFT_BLOCK, (blocks + 1) * LANES), BF16),
-            pltpu.SemaphoreType.DMA((8,)),
+            pltpu.SemaphoreType.DMA((7,)),
             pltpu.SemaphoreType.DMA((2, halves, groups)),
             pltpu.SemaphoreType.DMA((2, halves, groups)),
             pltpu.SemaphoreType.DMA((halves, FILTER_PARTS)),
@@ -402,9 +408,9 @@
             pltpu.SemaphoreType.DMA((3, halves, shards)),
         ],
         compiler_params=pltpu.CompilerParams(
-            collective_id=0, has_side_effects=True, vmem_limit_bytes=48 * 1024 * 1024
+            collective_id=0, has_side_effects=True, vmem_limit_bytes=61500 * 1024
         ),
-    )(ranks, first_length, q_arrive[0], k_arrive[0], v_arrive[0], filter_taps, *tables)
+    )(source_rank, first_length, q_arrive[0], k_arrive[0], v_arrive[0], filter_taps, tables)
     return result[None]
 
 

time: 51.7 us -> 43.1 us (0.83)
  local copies, waits for them, and re-layouts: 10.3 us -> 1.88 us
    unnamed x21 -> x1, local copies, waits for them, and re-layouts: 10.1 us -> 1.88 us
where the time goes in v3:
time: 43.1 us; the launch traced here: 42.9 us
  Pallas kernels  41 us (95%)
  local copies, waits for them, and re-layouts  1.88 us (4%)
    pallas_call x1, Pallas kernels, body(): pl.pallas_call(functools.partial(kernel, groups, shards, halves, rows, bl...  41 us
    unnamed x1, local copies, waits for them, and re-layouts  1.88 us

profile of v3, /device:TPU:1, one launch (start us, length us, event | category | flops | bytes accessed | tf_op | source)
XLA Modules:
  0.0 42.9 jit_solution(8923284682077021345)
XLA Ops:
  0.0 41.0 %shard_map.73 = bf16[128,2048]{1,0:T(8,128)(2,1)} custom-call(s32[4,32]{1,0:T(4,128)} %rank_hbm.1, s32[4]{0:T(128)} %first_hbm.1, bf16[128,2048]{1,0:T(8,128)(2,1)} %bitcast.5, bf16[128,2048]{1,0:T(8,128)(2,1)} %bitcast.6, bf16[128,2048]{1,0:T(8,128)(2,1)} %bitcast.7, bf16[128,2048]{1,0:T(8,128)(2,1)} %f_hbm.1, bf16[4,512,256]{2,1,0:T(8,128)(2,1)} %constant.2.clone.tables_hbm), custom_call_target="tpu_custom_call" | custom-call | tf_op jit(solution)/shard_map/pallas_call | solution.py:380
  41.0 1.9 %copy.9 = bf16[1,128,2048]{2,1,0:T(8,128)(2,1)} copy(bf16[1,128,2048]{2,1,0:T(8,128)(2,1)} %bitcast.4) | data formatting | bytes 1048576

commit v4 on v3

--- a/solution.py
+++ b/solution.py
@@ -175,7 +175,7 @@
             cols = lane_tile(tile * halves + half)
             return (k_ref[:, cols].astype(F32) * v_ref[:, cols].astype(F32)).astype(BF16)
 
-        @pl.loop(0, shards // 2)
+        @pl.loop(0, shards // 2, unroll=True)
         def _(tile):
             pack(0, half, tile, product)
 
@@ -185,7 +185,7 @@
     loads[3].wait()
     for half in range(halves):
 
-        @pl.loop(0, shards // 2)
+        @pl.loop(0, shards // 2, unroll=True)
         def _(tile):
             pack(1, half, tile, lambda t: q_ref[:, lane_tile(t * halves + half)])
 
@@ -205,13 +205,12 @@
     for half in range(halves):
         for j in range(1, groups):
             dp_copy(0, half, j).wait_recv()
+        for j in range(1, groups):
+            dp_copy(1, half, j).start()
         xsend[half] = jnp.dot(recv_pick, recv[0, half], preferred_element_type=F32).astype(BF16)
         for j in range(1, shards):
             z_copy(1, half, j).start()
         xbuf[half, my_rows(), :] = xsend[half, :, lane_tile(me_seq)]
-    for half in range(halves):
-        for j in range(1, groups):
-            dp_copy(1, half, j).start()
     for load in [loads[4], loads[6]]:
         load.wait()
     boundary = first_ref[me_dp]

time: 43.1 us -> 42.6 us (0.988)
    pallas_call x1, Pallas kernels: 41 us -> 40.6 us  [body(): pl.pallas_call(functools.partial(kernel, groups, shards, halves, rows, bl...]
where the time goes in v4:
time: 42.6 us; the launch traced here: 42.4 us
  Pallas kernels  40.6 us (95%)
  local copies, waits for them, and re-layouts  1.88 us (4%)
    pallas_call x1, Pallas kernels, body(): pl.pallas_call(functools.partial(kernel, groups, shards, halves, rows, bl...  40.6 us
    unnamed x1, local copies, waits for them, and re-layouts  1.88 us

profile of v4, /device:TPU:1, one launch (start us, length us, event | category | flops | bytes accessed | tf_op | source)
XLA Modules:
  0.0 42.4 jit_solution(656043288562449229)
XLA Ops:
  0.0 40.6 %shard_map.73 = bf16[128,2048]{1,0:T(8,128)(2,1)} custom-call(s32[4,32]{1,0:T(4,128)} %rank_hbm.1, s32[4]{0:T(128)} %first_hbm.1, bf16[128,2048]{1,0:T(8,128)(2,1)} %bitcast.5, bf16[128,2048]{1,0:T(8,128)(2,1)} %bitcast.6, bf16[128,2048]{1,0:T(8,128)(2,1)} %bitcast.7, bf16[128,2048]{1,0:T(8,128)(2,1)} %f_hbm.1, bf16[4,512,256]{2,1,0:T(8,128)(2,1)} %constant.2.clone.tables_hbm), custom_call_target="tpu_custom_call" | custom-call | tf_op jit(solution)/shard_map/pallas_call | solution.py:379
  40.6 1.9 %copy.9 = bf16[1,128,2048]{2,1,0:T(8,128)(2,1)} copy(bf16[1,128,2048]{2,1,0:T(8,128)(2,1)} %bitcast.4) | data formatting | bytes 1048576
